TPU v7x, 32 devices: a whole 2x2x4 slice. The times are simulated.
32 devices in a mesh: dp: 16 (over z, y, core), seq: 2 (over x).
Axes of the slice: x: 2, y: 2, z: 4, core: 2. Of those that a mesh axis runs over, the one named last changes fastest.
Arguments:
- tokens: bfloat16 [32, 1024, 768], P('dp', 'seq'), may hold values from -6 to 6
- lengths: int32 [32], P('dp'), may hold values from 256 to 1024, as said below
- key_mask: int32 [32, 1024], P('dp', 'seq'), may hold values 0 or 1
- attn_gain: float32 [768], replicated, may hold values from 0.5 to 1.5
- attn_shift: float32 [768], replicated, may hold values from -3 to 3
- w_qkv: bfloat16 [768, 2304], replicated, may hold values from -0.3125 to 0.3125
- query_bias: float32 [768], replicated, may hold values from -3 to 3
- value_bias: float32 [768], replicated, may hold values from -3 to 3
- w_out: bfloat16 [768, 768], replicated, may hold values from -0.4375 to 0.4375
- out_bias: float32 [768], replicated, may hold values from -3 to 3
- ffn_gain: float32 [768], replicated, may hold values from 0.5 to 1.5
- ffn_shift: float32 [768], replicated, may hold values from -3 to 3
- w_in: bfloat16 [768, 3072], replicated, may hold values from -0.21875 to 0.21875
- in_bias: float32 [3072], replicated, may hold values from -3 to 3
- w_back: bfloat16 [3072, 768], replicated, may hold values from -0.21875 to 0.21875
- back_bias: float32 [768], replicated, may hold values from -3 to 3
- cotangent: bfloat16 [32, 1024, 768], P('dp', 'seq'), may hold values from -40 to 40
Outputs:
- layer_out: bfloat16 [32, 1024, 768], P('dp', 'seq')
- grad_tokens: float32 [32, 1024, 768], P('dp', 'seq')
- grad_attn_gain: float32 [768], P(('dp', 'seq'))
- grad_attn_shift: float32 [768], P(('dp', 'seq'))
- grad_w_qkv: float32 [768, 2304], P(('dp', 'seq'))
- grad_query_bias: float32 [768], P(('dp', 'seq'))
- grad_value_bias: float32 [768], P(('dp', 'seq'))
- grad_w_out: float32 [768, 768], P(('dp', 'seq'))
- grad_out_bias: float32 [768], P(('dp', 'seq'))
- grad_ffn_gain: float32 [768], P(('dp', 'seq'))
- grad_ffn_shift: float32 [768], P(('dp', 'seq'))
- grad_w_in: float32 [768, 3072], P(('dp', 'seq'))
- grad_in_bias: float32 [3072], P(('dp', 'seq'))
- grad_w_back: float32 [3072, 768], P(('dp', 'seq'))
- grad_back_bias: float32 [768], P(('dp', 'seq'))
Inputs may be any that keep to these rules, and one draw needn't show every extreme that they name: `lengths`: in each aligned group of 2 sequences (those of one index of dp), one has length 1024.
All inputs are finite; a program needn't handle non-finite values. No bound on the sum of `key_mask` on one device may be relied on, other than what follows from the above.
Results may differ from a plain program's by a relative error of at most 0.023.
Values may be sent and summed in bfloat16 or wider, within the bound.
A program may use at most 256 MiB of HBM per device.

v0:
```python
import jax
import jax.numpy as jnp
from jax import lax
from jax.sharding import PartitionSpec as P

H = 12
HD = 64


NEG_FILL = -1e30
NORM_EPS = 1e-05


def shifted(array, axis, by):
    devices = lax.axis_size(axis)
    return lax.ppermute(array, axis, [(i, (i + by) % devices) for i in range(devices)])


def layer_norm(values, gain, shift):
    center = values - jnp.mean(values, axis=-1, keepdims=True)
    spread = jnp.mean(center * center, axis=-1, keepdims=True)
    return center * lax.rsqrt(spread + NORM_EPS) * gain + shift


def partial_gelu(values):
    return jax.nn.gelu(values, approximate=True)


def outer_product(left, right):
    return lax.dot_general(
        left, right, (((0,), (0,)), ((), ())), preferred_element_type=jnp.float32
    )


def times_transposed(left, right):
    return lax.dot_general(
        left, right, (((1,), (1,)), ((), ())), preferred_element_type=jnp.float32
    )


def allowed_keys(lengths, flags_all, query_pos, first_key, key_count):
    key_pos = first_key + jnp.arange(key_count, dtype=jnp.int32)
    key_flags = lax.dynamic_slice_in_dim(flags_all, first_key, key_count, 1)
    key_valid = (key_pos[None, :] < lengths[:, None]) & (key_flags == 1)
    itself = key_pos[None, :] == query_pos[:, None]
    return key_valid[:, None, None, :] | itself[None, :, None, :]


def send_home(partial_grads):
    return shifted(partial_grads.astype(jnp.bfloat16), "seq", 1).astype(partial_grads.dtype)


def shards(
    tokens,
    lengths,
    key_mask,
    attn_gain,
    attn_shift,
    w_qkv,
    query_bias,
    value_bias,
    w_out,
    out_bias,
    ffn_gain,
    ffn_shift,
    w_in,
    in_bias,
    w_back,
    back_bias,
    cotangent,
):
    seq_count, span_dev, model_width = tokens.shape
    row_count = seq_count * span_dev
    members = lax.axis_size("seq")
    own_index = lax.axis_index("seq")
    query_pos = own_index * span_dev + jnp.arange(span_dev, dtype=jnp.int32)
    flags_all = lax.all_gather(key_mask, "seq", axis=1, tiled=True)
    inputs = tokens.astype(jnp.float32).reshape(row_count, model_width)
    normed_one, norm_pull_one = jax.vjp(layer_norm, inputs, attn_gain, attn_shift)
    normed_attn = normed_one.astype(jnp.bfloat16)
    projected = jnp.dot(normed_attn, w_qkv, preferred_element_type=jnp.float32)
    queries = ((projected[:, :model_width] + query_bias) * 0.125).astype(jnp.bfloat16)
    queries = queries.reshape(seq_count, span_dev, H, HD)
    keyval = jnp.concatenate(
        [projected[:, model_width : 2 * model_width], projected[:, 2 * model_width :] + value_bias],
        axis=1,
    ).astype(jnp.bfloat16)
    keyval = keyval.reshape(seq_count, span_dev, 2 * model_width)

    def split_block(block_kv):
        key_count = block_kv.shape[1]
        key_heads = block_kv[:, :, :model_width].reshape(seq_count, key_count, H, HD)
        value_heads = block_kv[:, :, model_width:].reshape(seq_count, key_count, H, HD)
        return (key_count, key_heads, value_heads)

    running_max = jnp.full((seq_count, span_dev, H), NEG_FILL, jnp.float32)
    key_count, key_heads, value_heads = split_block(
        lax.all_gather(keyval, "seq", axis=1, tiled=True)
    )
    scores = jnp.einsum("sqhd,skhd->sqhk", queries, key_heads, preferred_element_type=jnp.float32)
    allowed = allowed_keys(lengths, flags_all, query_pos, jnp.int32(0), key_count)
    new_max = jnp.maximum(running_max, jnp.max(jnp.where(allowed, scores, NEG_FILL), axis=-1))
    expo = jnp.exp(jnp.where(allowed, scores - new_max[..., None], NEG_FILL))
    running_sum = jnp.sum(expo, axis=-1)
    running_acc = jnp.einsum(
        "sqhk,skhd->sqhd",
        expo.astype(jnp.bfloat16),
        value_heads,
        preferred_element_type=jnp.float32,
    )
    attended = running_acc / running_sum[..., None]
    log_total = new_max + jnp.log(running_sum)
    context = attended.reshape(row_count, model_width).astype(jnp.bfloat16)
    residual = inputs + jnp.dot(context, w_out, preferred_element_type=jnp.float32) + out_bias
    normed_two, norm_pull_two = jax.vjp(layer_norm, residual, ffn_gain, ffn_shift)
    normed_ffn = normed_two.astype(jnp.bfloat16)
    pre_act = jnp.dot(normed_ffn, w_in, preferred_element_type=jnp.float32) + in_bias
    gelu_value, gelu_pull = jax.vjp(partial_gelu, pre_act)
    activated = gelu_value.astype(jnp.bfloat16)
    layer_out = (
        residual + jnp.dot(activated, w_back, preferred_element_type=jnp.float32) + back_bias
    )
    grad_rows = cotangent.reshape(row_count, model_width)
    grad_float = grad_rows.astype(jnp.float32)
    grad_back_bias = jnp.sum(grad_float, axis=0)
    grad_w_back = outer_product(activated, grad_rows)
    d_act = times_transposed(grad_rows, w_back)
    d_pre = gelu_pull(d_act)[0].astype(jnp.bfloat16)
    grad_in_bias = jnp.sum(d_pre.astype(jnp.float32), axis=0)
    grad_w_in = outer_product(normed_ffn, d_pre)
    d_normed = times_transposed(d_pre, w_in)
    d_res_part, grad_ffn_gain, grad_ffn_shift = norm_pull_two(d_normed)
    d_residual = grad_float + d_res_part
    d_branch = d_residual.astype(jnp.bfloat16)
    grad_out_bias = jnp.sum(d_branch.astype(jnp.float32), axis=0)
    grad_w_out = outer_product(context, d_branch)
    d_attended = (
        times_transposed(d_branch, w_out).astype(jnp.bfloat16).reshape(seq_count, span_dev, H, HD)
    )
    delta = jnp.sum(d_attended.astype(jnp.float32) * attended, axis=-1)

    def attend_back(block_kv, first_key):
        key_count, key_heads, value_heads = split_block(block_kv)
        scores = jnp.einsum(
            "sqhd,skhd->sqhk", queries, key_heads, preferred_element_type=jnp.float32
        )
        allowed = allowed_keys(lengths, flags_all, query_pos, first_key, key_count)
        weights_f = jnp.exp(jnp.where(allowed, scores - log_total[..., None], NEG_FILL))
        d_values = jnp.einsum(
            "sqhk,sqhd->skhd",
            weights_f.astype(jnp.bfloat16),
            d_attended,
            preferred_element_type=jnp.float32,
        )
        d_probs = jnp.einsum(
            "sqhd,skhd->sqhk", d_attended, value_heads, preferred_element_type=jnp.float32
        )
        d_scores = (weights_f * (d_probs - delta[..., None])).astype(jnp.bfloat16)
        d_query = jnp.einsum(
            "sqhk,skhd->sqhd", d_scores, key_heads, preferred_element_type=jnp.float32
        )
        d_keys = jnp.einsum(
            "sqhk,sqhd->skhd", d_scores, queries, preferred_element_type=jnp.float32
        )
        d_block = jnp.concatenate(
            [
                d_keys.reshape(seq_count, key_count, model_width),
                d_values.reshape(seq_count, key_count, model_width),
            ],
            axis=2,
        )
        return (d_query, d_block)

    zero_query = jnp.zeros((seq_count, span_dev, H, HD), jnp.float32)

    def turn(turn_index, state_now):
        current, d_current, d_query = state_now
        anchor = (own_index - turn_index) % members
        add_query, add_block = attend_back(current, anchor * span_dev)
        current = shifted(current, "seq", 1)
        return (current, send_home(d_current + add_block), d_query + add_query)

    start_back = (
        keyval,
        jnp.zeros((seq_count, span_dev, 2 * model_width), jnp.float32),
        zero_query,
    )
    current, d_current, d_query = lax.fori_loop(0, members - 1, turn, start_back)
    anchor = (own_index - (members - 1)) % members
    add_query, add_block = attend_back(current, anchor * span_dev)
    d_query = d_query + add_query
    d_keyval = send_home(d_current + add_block)
    d_query_low = d_query.reshape(row_count, model_width).astype(jnp.bfloat16)
    d_keyval_low = d_keyval.reshape(row_count, 2 * model_width).astype(jnp.bfloat16)
    query_scaled = d_query_low.astype(jnp.float32) * 0.125
    grad_query_bias = jnp.sum(query_scaled, axis=0)
    grad_value_bias = jnp.sum(d_keyval_low[:, model_width:].astype(jnp.float32), axis=0)
    d_projected = jnp.concatenate([query_scaled.astype(jnp.bfloat16), d_keyval_low], axis=1)
    grad_w_qkv = outer_product(normed_attn, d_projected)
    d_normed_attn = times_transposed(d_projected, w_qkv)
    d_in_part, grad_attn_gain, grad_attn_shift = norm_pull_one(d_normed_attn)
    grad_tokens = (d_residual + d_in_part).reshape(seq_count, span_dev, model_width)
    out_block = layer_out.astype(jnp.bfloat16).reshape(seq_count, span_dev, model_width)
    all_sums = (
        lax.psum_scatter(grad_attn_gain, ("dp", "seq"), scatter_dimension=0, tiled=True),
        lax.psum_scatter(grad_attn_shift, ("dp", "seq"), scatter_dimension=0, tiled=True),
        lax.psum_scatter(grad_w_qkv, ("dp", "seq"), scatter_dimension=0, tiled=True),
        lax.psum_scatter(grad_query_bias, ("dp", "seq"), scatter_dimension=0, tiled=True),
        lax.psum_scatter(grad_value_bias, ("dp", "seq"), scatter_dimension=0, tiled=True),
        lax.psum_scatter(grad_w_out, ("dp", "seq"), scatter_dimension=0, tiled=True),
        lax.psum_scatter(grad_out_bias, ("dp", "seq"), scatter_dimension=0, tiled=True),
        lax.psum_scatter(grad_ffn_gain, ("dp", "seq"), scatter_dimension=0, tiled=True),
        lax.psum_scatter(grad_ffn_shift, ("dp", "seq"), scatter_dimension=0, tiled=True),
        lax.psum_scatter(grad_w_in, ("dp", "seq"), scatter_dimension=0, tiled=True),
        lax.psum_scatter(grad_in_bias, ("dp", "seq"), scatter_dimension=0, tiled=True),
        lax.psum_scatter(grad_w_back, ("dp", "seq"), scatter_dimension=0, tiled=True),
        lax.psum_scatter(grad_back_bias, ("dp", "seq"), scatter_dimension=0, tiled=True),
    )
    return (
        out_block,
        grad_tokens,
        all_sums[0],
        all_sums[1],
        all_sums[2],
        all_sums[3],
        all_sums[4],
        all_sums[5],
        all_sums[6],
        all_sums[7],
        all_sums[8],
        all_sums[9],
        all_sums[10],
        all_sums[11],
        all_sums[12],
    )


def solution(mesh):
    return jax.shard_map(
        shards,
        mesh=mesh,
        in_specs=(
            P("dp", "seq", None),
            P("dp"),
            P("dp", "seq"),
            P(),
            P(),
            P(),
            P(),
            P(),
            P(),
            P(),
            P(),
            P(),
            P(),
            P(),
            P(),
            P(),
            P("dp", "seq", None),
        ),
        out_specs=(
            P("dp", "seq", None),
            P("dp", "seq", None),
            P(("dp", "seq")),
            P(("dp", "seq")),
            P(("dp", "seq"), None),
            P(("dp", "seq")),
            P(("dp", "seq")),
            P(("dp", "seq"), None),
            P(("dp", "seq")),
            P(("dp", "seq")),
            P(("dp", "seq")),
            P(("dp", "seq"), None),
            P(("dp", "seq")),
            P(("dp", "seq"), None),
            P(("dp", "seq")),
        ),
        check_vma=False,
    )
```

profile of v0, /device:TPU:0, one launch (start us, length us, event | category | flops | bytes accessed | tf_op | source)
XLA Modules:
  0.0 771.4 jit_solution(2629363640464945292)
XLA Ops:
  13.1 3.8 fusion.97
  22.6 2.6 copy.88
  25.2 3.8 reshape.308
  29.1 5.4 all_gather.7
  36.9 68.8 %all-gather.2.cloned.1.call-done = bf16[2,1024,1536]{2,1,0:T(8,128)(2,1)} async-done(((bf16[2,512,1536]{2,1,0:T(8,128)(2,1)}), bf16[2,1024,1536]{2,1,0:T(8,128)(2,1)}) %all-gather.2.cloned.1.call-update) | async-done | bytes 6291472 | tf_op jit(solution)/shard_map/all_gather | solution.py:98
  105.7 6.0 fusion.93
  111.7 4.7 copy.87
  116.4 20.1 %fusion = (f32[2,512,12]{1,2,0:T(8,128)S(1)}, f32[2,12,1024,512]{3,2,1,0:T(8,128)}) fusion(pred[2,512,1024]{1,2,0:T(8,128)(4,1)} %broadcast_or_fusion, bf16[2,1024,12,64]{1,3,2,0:T(8,128)(2,1)} %bitcast.173, bf16[2,512,12,64]{1,0,3,2:T(2,128)(2,1)} %reshape.308), kind=kOutput, calls=%fused_computation.2 | convolution fusion | flops 1635766272 | bytes 56147968 | tf_op jit(solution)/shard_map/sqhd,skhd->sqhk/dot_general | solution.py:100
  137.7 4.7 copy.86
  142.4 21.2 %fusion.3 = f32[2,512,12]{1,2,0:T(8,128)S(1)} fusion(f32[2,12,1024,512]{3,2,1,0:T(8,128)} %get-tuple-element.89, f32[2,512,12]{1,2,0:T(8,128)} %broadcast_maximum_fusion, pred[2,512,1024]{1,2,0:T(8,128)(4,1)} %broadcast_or_fusion), kind=kLoop, calls=%fused_computation.5 | loop fusion | flops 37736448 | bytes 51478528 | tf_op jit(solution)/shard_map/reduce_sum | solution.py:104
  163.6 20.4 %fusion.95 = (bf16[2,512,12,64]{1,3,2,0:T(8,128)(2,1)S(1)}, f32[2,512,12,64]{1,3,2,0:T(8,128)}) fusion(f32[2,512,12]{1,2,0:T(8,128)S(1)} %fusion.3, bf16[2,1024,12,64]{1,3,2,0:T(8,128)(2,1)S(1)} %bitcast.178, f32[2,12,1024,512]{3,2,1,0:T(8,128)} %get-tuple-element.89, f32[2,512,12]{1,2,0:T(8,128)S(1)} %copy-done.25, pred[2,512,1024]{1,2,0:T(8,128)(4,1)S(1)} %copy-done.9), kind=kOutput, calls=%fused_computation.148 | convolution fusion | flops 1649934336 | bytes 59342848 | tf_op jit(solution)/shard_map/sqhk,skhd->sqhd/dot_general | solution.py:105
  188.8 8.6 %fusion.88 = f32[1024,3072]{1,0:T(8,128)} fusion(bf16[768,3072]{1,0:T(8,128)(2,1)S(1)} %bitcast.191, f32[1024,768]{1,0:T(8,128)S(1)} %get-tuple-element.93, f32[768]{0:T(1024)S(1)} %copy-done.31, f32[768]{0:T(1024)S(1)} %copy-done.26, f32[1024]{0:T(1024)S(1)} %fusion.79, f32[1024]{0:T(1024)S(1)} %broadcast_multiply_fusion), kind=kOutput, calls=%fused_computation.142 | convolution fusion | flops 4835770368 | bytes 20461568 | tf_op jit(solution)/shard_map/dot_general | solution.py:117
  197.4 15.6 %convert_reduce_fusion = (f32[3072]{0:T(1024)}, bf16[1024,3072]{1,0:T(8,128)(2,1)S(1)}) fusion(f32[1024,3072]{1,0:T(8,128)} %fusion.88, f32[3072]{0:T(1024)S(1)} %copy-done.46, bf16[1024,768]{1,0:T(8,128)(2,1)S(1)} %bitcast.169, bf16[3072,768]{1,0:T(8,128)(2,1)} %param.31), kind=kOutput, calls=%fused_computation.34 | convolution fusion | flops 4904186880 | bytes 25190400 | tf_op jit(solution)/shard_map/dot_general | solution.py:36
  213.0 10.9 %multiply_reduce_fusion = (f32[768]{0:T(1024)}, f32[1024]{0:T(1024)S(1)}, f32[768]{0:T(1024)}, f32[1024,768]{1,0:T(8,128)S(1)}) fusion(f32[1024,768]{1,0:T(8,128)S(1)} %get-tuple-element.93, f32[1024]{0:T(1024)S(1)} %fusion.79, f32[1024]{0:T(1024)S(1)} %broadcast_multiply_fusion, f32[768]{0:T(1024)S(1)} %copy-done.26, ...), kind=kOutput, calls=%fused_computation.73 | convolution fusion | flops 4838126592 | bytes 17323008 | tf_op jit(solution)/shard_map/dot_general | solution.py:36
  228.4 2.8 fusion.98
  231.2 11.3 %fusion.87 = f32[768,3072]{1,0:T(8,128)} fusion(bf16[1024,3072]{1,0:T(8,128)(2,1)} %copy-done.15, f32[1024,768]{1,0:T(8,128)} %copy-done.5, f32[768]{0:T(1024)} %param.28, f32[768]{0:T(1024)} %param.27, f32[1024]{0:T(1024)S(1)} %fusion.79, f32[1024]{0:T(1024)S(1)} %broadcast_multiply_fusion), kind=kOutput, calls=%fused_computation.141 | convolution fusion | flops 4835770368 | bytes 18888704 | tf_op jit(solution)/shard_map/dot_general | solution.py:30
  242.9 2.6 copy.92
  245.5 2.6 copy.95
  248.1 3.9 reshape.311
  252.0 3.9 reshape.312
  258.6 11.9 %fusion.63 = f32[2,12,512,512]{3,2,1,0:T(8,128)} fusion(bf16[2,512,12,64]{1,0,3,2:T(2,128)(2,1)} %reshape.311, bf16[2,512,12,64]{1,0,3,2:T(2,128)(2,1)S(1)} %copy-done.1), kind=kOutput, calls=%fused_computation.97 | convolution fusion | flops 805306368 | bytes 28311552 | tf_op jit(solution)/shard_map/while/body/eval_jaxpr/sqhd,skhd->sqhk/dot_general | solution.py:144
  270.5 47.5 %collective-permute-done = bf16[2,512,1536]{2,1,0:T(8,128)(2,1)} collective-permute-done((bf16[2,512,1536]{2,1,0:T(8,128)(2,1)}, bf16[2,512,1536]{2,1,0:T(8,128)(2,1)}, u32[]{:S(2)}, u32[]{:S(2)}) %collective-permute-start) | collective-permute-done | bytes 3145760 | tf_op jit(solution)/shard_map/while/body/eval_jaxpr/ppermute | solution.py:16
  318.0 3.8 fusion.94
  324.4 2.6 copy.104
  327.1 13.8 %fusion.74 = f32[2,12,512,512]{3,2,1,0:T(8,128)} fusion(bf16[2,512,12,64]{1,3,2,0:T(8,128)(2,1)} %bitcast.165, bf16[2,512,12,64]{1,0,3,2:T(2,128)(2,1)} %reshape.308), kind=kOutput, calls=%fused_computation.110 | convolution fusion | flops 805306368 | bytes 28311552 | tf_op jit(solution)/shard_map/sqhd,skhd->sqhk/dot_general | solution.py:144
  346.1 3.9 reshape.313
  351.5 13.9 %fusion.89 = f32[3072,768]{1,0:T(8,128)} fusion(bf16[1024,768]{1,0:T(8,128)(2,1)} %bitcast.168, f32[1024,3072]{1,0:T(8,128)} %fusion.88, f32[3072]{0:T(1024)S(1)} %copy-done.47), kind=kOutput, calls=%fused_computation.143 | convolution fusion | flops 4863295488 | bytes 23605248 | tf_op jit(solution)/shard_map/dot_general | solution.py:30
  365.4 13.8 %fusion.58 = bf16[2,12,64,512]{3,2,1,0:T(8,128)(2,1)} fusion(f32[2,12,512,512]{3,2,1,0:T(8,128)} %fusion.63, f32[2,512,12]{1,2,0:T(8,128)} %log_add_fusion, pred[2,512,512]{1,2,0:T(8,128)(4,1)} %get-tuple-element.99, bf16[2,512,12,64]{1,0,3,2:T(2,128)(2,1)} %reshape.313), kind=kOutput, calls=%fused_computation.92 | convolution fusion | flops 824967168 | bytes 28884992 | tf_op jit(solution)/shard_map/while/body/eval_jaxpr/sqhk,sqhd->skhd/dot_general | solution.py:149
  381.9 3.8 multiply_reduce_fusion.1
  385.6 16.4 %fusion.10 = bf16[2,512,12,512]{1,3,2,0:T(8,128)(2,1)} fusion(f32[2,12,512,512]{3,2,1,0:T(8,128)} %fusion.63, f32[2,512,12]{1,2,0:T(8,128)} %multiply_reduce_fusion.1, f32[2,512,12]{1,2,0:T(8,128)} %log_add_fusion, pred[2,512,512]{1,2,0:T(8,128)(4,1)} %get-tuple-element.99, bf16[2,512,12,64]{1,0,3,2:T(2,128)(2,1)} %reshape.312, ...), kind=kOutput, calls=%fused_computation.15 | convolution fusion | flops 836763648 | bytes 41517056 | tf_op jit(solution)/shard_map/while/body/eval_jaxpr/sqhd,skhd->sqhk/dot_general | solution.py:155
  402.0 10.2 %convolution_convert_fusion = bf16[2,12,64,512]{3,2,1,0:T(8,128)(2,1)} fusion(bf16[2,512,12,512]{1,3,2,0:T(8,128)(2,1)} %fusion.10, bf16[2,512,12,64]{1,0,3,2:T(2,128)(2,1)} %reshape.308), kind=kOutput, calls=%fused_computation.93 | convolution fusion | flops 806092800 | bytes 15728640 | tf_op jit(solution)/shard_map/while/body/eval_jaxpr/sqhk,sqhd->skhd/dot_general | solution.py:162
  412.2 2.6 copy.112
  414.8 3.9 pad_maximum_fusion.2
  418.8 13.4 %fusion.25 = f32[2,12,64,512]{3,2,1,0:T(8,128)} fusion(f32[2,12,512,512]{3,2,1,0:T(8,128)} %fusion.74, f32[2,512,12]{1,2,0:T(8,128)S(1)} %copy-done.24, pred[2,512,512]{1,2,0:T(8,128)(4,1)S(1)} %copy-done.17, bf16[2,512,12,64]{1,0,3,2:T(2,128)(2,1)S(1)} %copy-done.13), kind=kOutput, calls=%fused_computation.32 | convolution fusion | flops 824180736 | bytes 30457856 | tf_op jit(solution)/shard_map/sqhk,sqhd->skhd/dot_general | solution.py:149
  432.2 3.6 copy.119
  435.8 16.2 %fusion.6 = bf16[2,512,12,512]{1,3,2,0:T(8,128)(2,1)} fusion(f32[2,12,512,512]{3,2,1,0:T(8,128)} %fusion.74, f32[2,512,12]{1,2,0:T(8,128)} %multiply_reduce_fusion.1, f32[2,512,12]{1,2,0:T(8,128)} %log_add_fusion, pred[2,512,512]{1,2,0:T(8,128)(4,1)} %get-tuple-element.98, bf16[2,512,12,64]{1,3,2,0:T(8,128)(2,1)} %bitcast.180, ...), kind=kOutput, calls=%fused_computation.9 | convolution fusion | flops 836763648 | bytes 41517056 | tf_op jit(solution)/shard_map/sqhd,skhd->sqhk/dot_general | solution.py:155
  452.0 10.7 %fusion.71 = f32[2,12,64,512]{3,2,1,0:T(8,128)} fusion(bf16[2,512,12,512]{1,3,2,0:T(8,128)(2,1)} %fusion.6, bf16[2,512,12,64]{1,0,3,2:T(2,128)(2,1)} %reshape.308), kind=kOutput, calls=%fused_computation.107 | convolution fusion | flops 805306368 | bytes 17301504 | tf_op jit(solution)/shard_map/sqhk,sqhd->skhd/dot_general | solution.py:162
  462.7 3.7 copy.118
  466.4 34.0 %collective-permute-done.1 = bf16[2,512,1536]{2,1,0:T(8,128)(2,1)} collective-permute-done((bf16[2,512,1536]{2,1,0:T(8,128)(2,1)}, bf16[2,512,1536]{2,1,0:T(8,128)(2,1)}, u32[]{:S(2)}, u32[]{:S(2)}) %collective-permute-start.1) | collective-permute-done | bytes 3145760 | tf_op jit(solution)/shard_map/while/body/eval_jaxpr/ppermute | solution.py:16
  500.4 6.9 fusion.35
  507.9 7.6 fusion.65
  523.8 69.9 %collective-permute-done.2 = bf16[2,512,1536]{2,1,0:T(8,128)(2,1)} collective-permute-done((bf16[2,512,1536]{2,1,0:T(8,128)(2,1)}, bf16[2,512,1536]{2,1,0:T(8,128)(2,1)}, u32[]{:S(2)}, u32[]{:S(2)}) %collective-permute-start.2) | collective-permute-done | bytes 3145760 | tf_op jit(solution)/shard_map/ppermute | solution.py:16
  593.7 9.6 %fusion.53 = f32[768,2304]{1,0:T(8,128)} fusion(bf16[1024,768]{1,0:T(8,128)(2,1)} %copy-done.18, bf16[1024,1536]{1,0:T(8,128)(2,1)} %bitcast.24, bf16[1024,768]{1,0:T(8,128)(2,1)} %copy.120), kind=kOutput, calls=%fused_computation.87 | convolution fusion | flops 3633315840 | bytes 13369344 | tf_op jit(solution)/shard_map/dot_general | solution.py:30
  606.2 13.8 %add_convert_fusion.1 = bf16[1024,768]{1,0:T(8,128)(2,1)} fusion(f32[1024,768]{1,0:T(8,128)} %copy-done.5, bf16[3072,768]{1,0:T(8,128)(2,1)} %param.31, f32[768]{0:T(1024)S(1)} %copy-done.49, f32[1024,3072]{1,0:T(8,128)} %fusion.88, f32[3072]{0:T(1024)} %param.30), kind=kOutput, calls=%fused_computation.84 | convolution fusion | flops 4865654784 | bytes 22035456 | tf_op jit(solution)/shard_map/dot_general | solution.py:121
  622.4 6.6 fusion.90
  631.3 40.4 %all-reduce.9 = (f32[768]{0:T(1024)}, f32[768]{0:T(1024)}, f32[768]{0:T(1024)}, f32[768]{0:T(1024)}, f32[768]{0:T(1024)}, /*index=5*/f32[768]{0:T(1024)}, f32[768]{0:T(1024)}, f32[3072]{0:T(1024)}, f32[768]{0:T(1024)}) all-reduce(f32[768]{0:T(1024)} %get-tuple-element.56, ...), channel_id=2, replica_groups=mesh['dp'=16,'seq'=2] {'dp','seq'}, use_global_device_ids=true, to_apply=%region_12.13.clone | all-reduce | flops 9216 | bytes 73728
  683.7 5.8 add_add_fusion.2
  689.6 75.0 %reduce-scatter.5.cloned.1.call-done = f32[24,2304]{1,0:T(8,128)} async-done(((f32[768,2304]{1,0:T(8,128)}), f32[24,2304]{1,0:T(8,128)}) %reduce-scatter.5.cloned.1.call-update) | async-done | bytes 221200 | tf_op jit(solution)/shard_map/reduce_scatter | solution.py:207
  (183 shorter events, 68.0 us)
Async XLA Ops:
  7.2 5.9 copy-start
  7.2 5.2 copy-start.39
  7.2 5.2 copy-start.32
  7.2 98.5 %all-gather.2.cloned.1.call-start = ((), (), s32[]{:S(2)}) async-start(), calls=%async_computation.4 | async-start | bytes 9437184 | tf_op jit(solution)/shard_map/all_gather | solution.py:98
  7.3 5.2 copy-start.2
  13.1 3.9 copy-start.18
  22.5 667.1 %reduce-scatter.7.cloned.1.call-start = ((), (), s32[]{:S(2)}) async-start(), calls=%async_computation.6 | async-start | bytes 2433024 | tf_op jit(solution)/shard_map/reduce_scatter | solution.py:210
  22.6 6.5 copy-start.42
  22.6 11.9 %copy-start.43 = (s32[2]{0:T(128)S(1)}, s32[2]{0:T(128)}, u32[]{:S(2)}) copy-start(s32[2]{0:T(128)} %param.18) | copy-start | bytes 28
  142.4 21.2 %copy-start.9 = (pred[2,512,1024]{1,2,0:T(8,128)(4,1)S(1)}, pred[2,512,1024]{1,2,0:T(8,128)(4,1)}, u32[]{:S(2)}) copy-start(pred[2,512,1024]{1,2,0:T(8,128)(4,1)} %broadcast_or_fusion) | copy-start | bytes 3145732
  142.4 21.2 %copy-start.16 = (bf16[2,1024,768]{1,2,0:T(8,128)(2,1)S(1)}, bf16[2,1024,768]{1,2,0:T(8,128)(2,1)}, u32[]{:S(2)}) copy-start(bf16[2,1024,768]{1,2,0:T(8,128)(2,1)} %copy.86) | copy-start | bytes 9437188
  142.4 21.2 %copy-start.25 = (f32[2,512,12]{1,2,0:T(8,128)S(1)}, f32[2,512,12]{1,2,0:T(8,128)}, u32[]{:S(2)}) copy-start(f32[2,512,12]{1,2,0:T(8,128)} %broadcast_maximum_fusion) | copy-start | bytes 147460
  163.6 20.5 %copy-start.23 = (f32[2,512,12]{1,2,0:T(8,128)}, f32[2,512,12]{1,2,0:T(8,128)S(1)}, u32[]{:S(2)}) copy-start(f32[2,512,12]{1,2,0:T(8,128)S(1)} %fusion.3) | copy-start | bytes 147460
  184.0 2.1 copy-start.44
  184.0 2.1 copy-start.48
  186.1 2.3 slice-start.3
  186.1 2.3 slice-start.4
  187.8 36.0 %copy-start.5 = (f32[1024,768]{1,0:T(8,128)}, f32[1024,768]{1,0:T(8,128)S(1)}, u32[]{:S(2)}) copy-start(f32[1024,768]{1,0:T(8,128)S(1)} %get-tuple-element.93) | copy-start | bytes 9437188
  188.8 8.6 %copy-start.11 = (bf16[2,512,768]{2,1,0:T(8,128)(2,1)S(1)}, bf16[2,512,768]{2,1,0:T(8,128)(2,1)}, u32[]{:S(2)}) copy-start(bf16[2,512,768]{2,1,0:T(8,128)(2,1)} %param.33) | copy-start | bytes 4718596
  188.8 8.6 %copy-start.46 = (f32[3072]{0:T(1024)S(1)}, f32[3072]{0:T(1024)}, u32[]{:S(2)}) copy-start(f32[3072]{0:T(1024)} %param.30) | copy-start | bytes 36868
  213.0 10.9 %copy-start.15 = (bf16[1024,3072]{1,0:T(8,128)(2,1)}, bf16[1024,3072]{1,0:T(8,128)(2,1)S(1)}, u32[]{:S(2)}) copy-start(bf16[1024,3072]{1,0:T(8,128)(2,1)S(1)} %get-tuple-element.97) | copy-start | bytes 18874372
  231.2 458.4 %reduce-scatter.9.cloned.1.call-start = ((), (), s32[]{:S(2)}) async-start(), calls=%async_computation.7 | async-start | bytes 9732096 | tf_op jit(solution)/shard_map/reduce_scatter | solution.py:214
  242.5 447.1 %reduce-scatter.11.cloned.1.call-start = ((), (), s32[]{:S(2)}) async-start(), calls=%async_computation.8 | async-start | bytes 9732096 | tf_op jit(solution)/shard_map/reduce_scatter | solution.py:216
  242.5 75.5 %collective-permute-start = (bf16[2,512,1536]{2,1,0:T(8,128)(2,1)}, bf16[2,512,1536]{2,1,0:T(8,128)(2,1)}, u32[]{:S(2)}, u32[]{:S(2)}) collective-permute-start(bf16[2,512,1536]{2,1,0:T(8,128)(2,1)} %pad_maximum_fusion.1), channel_id=1, source_target_pairs={{0,1},{1,0},{2,3},{3,2},{4,5},{5,4},{6,7},{7,6},{8,9},{9,8},{10,11... | collective-permute-start | bytes 9437192 | tf_op jit(solution)/shard_map/while/body/eval_jaxpr/ppermute | solution.py:16
  248.1 8.6 %copy-start.38 = (s32[512]{0:T(512)S(1)}, s32[512]{0:T(512)}, u32[]{:S(2)}) copy-start(s32[512]{0:T(512)} %copy-done.37) | copy-start | bytes 6148
  255.9 2.7 copy-start.1
  327.0 13.8 %copy-start.21 = (bf16[1024,768]{1,0:T(8,128)(2,1)S(1)}, bf16[1024,768]{1,0:T(8,128)(2,1)}, u32[]{:S(2)}) copy-start(bf16[1024,768]{1,0:T(8,128)(2,1)} %copy-done.20) | copy-start | bytes 4718596
  327.1 13.8 %copy-start.45 = (bf16[768,768]{1,0:T(8,128)(2,1)S(1)}, bf16[768,768]{1,0:T(8,128)(2,1)}, u32[]{:S(2)}) copy-start(bf16[768,768]{1,0:T(8,128)(2,1)} %param.25) | copy-start | bytes 3538948
  343.5 8.0 %copy-start.47 = (f32[3072]{0:T(1024)S(1)}, f32[3072]{0:T(1024)}, u32[]{:S(2)}) copy-start(f32[3072]{0:T(1024)} %param.30) | copy-start | bytes 36868
  365.4 399.2 %reduce-scatter.5.cloned.1.call-start = ((), (), s32[]{:S(2)}) async-start(), calls=%async_computation.5 | async-start | bytes 7299072 | tf_op jit(solution)/shard_map/reduce_scatter | solution.py:207
  414.8 4.0 copy-start.13
  414.8 4.0 copy-start.17
  414.8 4.0 copy-start.24
  418.7 81.8 %collective-permute-start.1 = (bf16[2,512,1536]{2,1,0:T(8,128)(2,1)}, bf16[2,512,1536]{2,1,0:T(8,128)(2,1)}, u32[]{:S(2)}, u32[]{:S(2)}) collective-permute-start(bf16[2,512,1536]{2,1,0:T(8,128)(2,1)} %pad_maximum_fusion.2), channel_id=1, source_target_pairs={{0,1},{1,0},{2,3},{3,2},{4,5},{5,4},{6,7},{7,6},{8,9},{9,8},{10,11... | collective-permute-start | bytes 9437192 | tf_op jit(solution)/shard_map/while/body/eval_jaxpr/ppermute | solution.py:16
  466.4 41.4 %copy-start.8 = (bf16[2,512,12,64]{1,0,3,2:T(2,128)(2,1)S(1)}, bf16[2,512,12,64]{1,0,3,2:T(2,128)(2,1)}, u32[]{:S(2)}) copy-start(bf16[2,512,12,64]{1,0,3,2:T(2,128)(2,1)} %reshape.311) | copy-start | bytes 4718596
  500.4 15.0 %slice-start = ((s8[12582912]{0:T(1024)(128)(4,1)}), s8[4194304]{0:T(1024)(128)(4,1)S(1)}, s32[]{:S(2)}) async-start(s8[12582912]{0:T(1024)(128)(4,1)} %bitcast.163), calls=%async_computation.9 | async-start | bytes 8388608
  507.3 8.1 %slice-start.1 = ((s8[12582912]{0:T(1024)(128)(4,1)}), s8[4194304]{0:T(1024)(128)(4,1)S(1)}, s32[]{:S(2)}) async-start(s8[12582912]{0:T(1024)(128)(4,1)} %bitcast.163), calls=%async_computation.10 | async-start | bytes 8388608
  507.3 8.1 %slice-start.2 = ((s8[12582912]{0:T(1024)(128)(4,1)}), s8[4194304]{0:T(1024)(128)(4,1)S(1)}, s32[]{:S(2)}) async-start(s8[12582912]{0:T(1024)(128)(4,1)} %bitcast.163), calls=%async_computation.11 | async-start | bytes 8388608
  507.3 8.5 %copy-start.7 = (bf16[2,512,768]{1,2,0:T(8,128)(2,1)S(1)}, bf16[2,512,768]{1,2,0:T(8,128)(2,1)}, u32[]{:S(2)}) copy-start(bf16[2,512,768]{1,2,0:T(8,128)(2,1)} %copy.102) | copy-start | bytes 4718596
  507.3 86.4 %collective-permute-start.2 = (bf16[2,512,1536]{2,1,0:T(8,128)(2,1)}, bf16[2,512,1536]{2,1,0:T(8,128)(2,1)}, u32[]{:S(2)}, u32[]{:S(2)}) collective-permute-start(bf16[2,512,1536]{2,1,0:T(8,128)(2,1)} %fusion.35), channel_id=1, source_target_pairs={{0,1},{1,0},{2,3},{3,2},{4,5},{5,4},{6,7},{7,6},{8,9},{9,8},{10,11... | collective-permute-start | bytes 9437192 | tf_op jit(solution)/shard_map/ppermute | solution.py:16
  603.2 3.0 copy-start.49
  606.2 16.1 %copy-start.4 = (bf16[2,512,768]{2,1,0:T(8,128)(2,1)S(1)}, bf16[2,512,768]{2,1,0:T(8,128)(2,1)}, u32[]{:S(2)}) copy-start(bf16[2,512,768]{2,1,0:T(8,128)(2,1)} %param.17) | copy-start | bytes 4718596
  606.2 16.1 %copy-start.19 = (bf16[1024,768]{1,0:T(8,128)(2,1)S(1)}, bf16[1024,768]{1,0:T(8,128)(2,1)}, u32[]{:S(2)}) copy-start(bf16[1024,768]{1,0:T(8,128)(2,1)} %copy.120) | copy-start | bytes 4718596
  606.2 16.1 %copy-start.30 = (f32[1,4,2,128]{3,1,2,0:T(4,128)S(1)}, f32[1,4,2,128]{3,1,2,0:T(4,128)}, u32[]{:S(2)}) copy-start(f32[1,4,2,128]{3,1,2,0:T(4,128)} %copy-done.29) | copy-start | bytes 12292
  606.2 16.1 %copy-start.33 = (f32[768]{0:T(1024)S(1)}, f32[768]{0:T(1024)}, u32[]{:S(2)}) copy-start(f32[768]{0:T(1024)} %param.20) | copy-start | bytes 9220
  622.4 6.6 copy-start.36
  622.4 6.6 copy-start.28
  629.0 2.3 copy-start.14
  (15 other events, 15.9 us)
Sparse Core Ops, SparseCore 0:
  22.6 83.0 all-gather.1
  231.3 103.2 reduce-scatter.6
  342.0 142.3 reduce-scatter.8
  490.8 148.5 reduce-scatter.10
  646.4 118.1 reduce-scatter.4
where the time goes:
time: 778 us; the launch traced here: 771 us
  waiting for transfers between devices  295 us (38%)
  matrix products  258 us (33%)
  local copies, waits for them, and re-layouts  88.7 us (11%)
  other arithmetic  67.9 us (9%)
  blocking collectives  45.8 us (6%)
  between operations  14.6 us (2%)
    ppermute x3, waiting for transfers between devices, shifted(): lax.ppermute(array, axis, [(i, (i + by) % devices) for i in range(devices)])  151 us
    reduce_scatter x1, waiting for transfers between devices, shards(): lax.psum_scatter(grad_w_qkv, ('dp', 'seq'), scatter_dimension=0, tiled=True)  75 us
    all_gather x1, waiting for transfers between devices, shards(): lax.all_gather(keyval, 'seq', axis=1, tiled=True)  68.8 us
    unnamed x1, blocking collectives  40.4 us
    dot_general x4, matrix products, outer_product(): lax.dot_general(left, right, (((0,), (0,)), ((), ())), preferred_element_...  37.5 us
    dot_general x4, matrix products, times_transposed(): lax.dot_general(left, right, (((1,), (1,)), ((), ())), preferred_element_...  35.6 us
    dot_general x2, matrix products, attend_back(): jnp.einsum('sqhd,skhd->sqhk', d_attended, value_heads, preferred_element_...  32.6 us
    dot_general x2, matrix products, attend_back(): jnp.einsum('sqhk,sqhd->skhd', weights_f.astype(jnp.bfloat16), d_attended,...  27.2 us
  transfers between devices with their start and end apart: 8, of which 5 were waited for; matrix products, arithmetic and copies ran while one was open for 35% of the time, Pallas kernels for 0%

commit v1 on v0

--- a/solution.py
+++ b/solution.py
@@ -1,6 +1,10 @@
+import functools
+
 import jax
 import jax.numpy as jnp
 from jax import lax
+from jax.experimental import pallas as pl
+from jax.experimental.pallas import tpu as pltpu
 from jax.sharding import PartitionSpec as P
 
 H = 12
@@ -9,6 +13,550 @@
 
 NEG_FILL = -1e30
 NORM_EPS = 1e-05
+
+F32 = jnp.float32
+BF16 = jnp.bfloat16
+D = 768
+FF = 3072
+T = 1024
+HALF = 512
+PAIRS = 6
+UNITS = 12
+UW = 384
+MESH = pl.DeviceIdType.MESH
+VMEM_LIMIT = 60 * 1024 * 1024
+
+
+def dot_nn(a, b):
+    return lax.dot_general(a, b, (((1,), (0,)), ((), ())), preferred_element_type=F32)
+
+
+def dot_nt(a, b):
+    return lax.dot_general(a, b, (((1,), (1,)), ((), ())), preferred_element_type=F32)
+
+
+def dot_tn(a, b):
+    return lax.dot_general(a, b, (((0,), (0,)), ((), ())), preferred_element_type=F32)
+
+
+def norm_parts(x):
+    center = x - jnp.mean(x, axis=-1, keepdims=True)
+    spread = jnp.mean(center * center, axis=-1, keepdims=True)
+    rstd = lax.rsqrt(spread + NORM_EPS)
+    return center * rstd, rstd
+
+
+def norm_back(d_norm, n, rstd, gain):
+    u = d_norm * gain
+    mean_u = jnp.mean(u, axis=-1, keepdims=True)
+    mean_un = jnp.mean(u * n, axis=-1, keepdims=True)
+    return (u - mean_u - n * mean_un) * rstd
+
+
+def fwd_kernel(
+    len_ref, mask_ref, tok_ref, gain_ref, shift_ref, w_ref, qb_ref, vb_ref,
+    nt_ref, q_ref, k_ref, v_ref, ctx_ref, lt_ref,
+):
+    @pl.loop(0, 4)
+    def _(t):
+        rows = pl.ds(pl.multiple_of(t * 256, 256), 256)
+        n, _ = norm_parts(tok_ref[rows, :].astype(F32))
+        normed = (n * gain_ref[...] + shift_ref[...]).astype(BF16)
+        nt_ref[:, rows] = normed.T
+        q_ref[rows, :] = ((dot_nn(normed, w_ref[:, :D]) + qb_ref[...]) * 0.125).astype(BF16)
+        k_ref[rows, :] = dot_nn(normed, w_ref[:, D : 2 * D]).astype(BF16)
+        v_ref[rows, :] = (dot_nn(normed, w_ref[:, 2 * D :]) + vb_ref[...]).astype(BF16)
+
+    pos = lax.broadcasted_iota(jnp.int32, (1, T), 1)
+    valid = (pos < len_ref[0]) & (mask_ref[...] == 1)
+    bias = jnp.where(valid, 0.0, NEG_FILL).astype(F32)
+    lane = lax.broadcasted_iota(jnp.int32, (1, 128), 1)
+    eye = lax.broadcasted_iota(jnp.int32, (256, 256), 0) == lax.broadcasted_iota(
+        jnp.int32, (256, 256), 1
+    )
+
+    @pl.loop(0, PAIRS)
+    def _(p):
+        cols = pl.ds(pl.multiple_of(p * 128, 128), 128)
+        kp = k_ref[:, cols]
+        vext = jnp.concatenate([v_ref[:, cols], jnp.ones((T, 128), BF16)], axis=1)
+        kh = [jnp.where((lane < HD) == (h == 0), kp, jnp.zeros_like(kp)) for h in range(2)]
+        for i in range(4):
+            qi = q_ref[i * 256 : (i + 1) * 256, cols]
+            outs = []
+            for h in range(2):
+                raw = dot_nt(qi, kh[h])
+                pieces = []
+                for j in range(4):
+                    cut = slice(j * 256, (j + 1) * 256)
+                    piece = raw[:, cut] + bias[:, cut]
+                    if i == j:
+                        piece = jnp.where(eye, raw[:, cut], piece)
+                    pieces.append(piece)
+                s = jnp.concatenate(pieces, axis=1)
+                top = jnp.max(s, axis=1, keepdims=True)
+                e = jnp.exp(s - top).astype(BF16)
+                o = dot_nn(e, vext)
+                total = o[:, 128:]
+                outs.append(o[:, :128] / total)
+                log_total = top + jnp.log(total)
+                lt_ref[2 * p + h, :, i * 256 : (i + 1) * 256] = log_total.T[0:1, :]
+            ctx_ref[i * 256 : (i + 1) * 256, cols] = jnp.where(lane < HD, outs[0], outs[1]).astype(BF16)
+
+
+def blocks_of(top, bottom):
+    return jnp.concatenate([top, bottom], axis=0).astype(BF16)
+
+
+def place(index, first_x):
+    z, y, c, x = index // 8, (index // 4) % 2, (index // 2) % 2, index % 2
+    return c * 16 + z + 4 * (2 * y + x) + first_x * 4 * (x - y)
+
+
+def ffn_kernel(
+    tok_ref, cot_ref, ctx_ref, wo_ref, ob_ref, g_ref, s_ref, wi_ref, ib_ref, wb_ref, bb_ref,
+    out_ref, dres_ref, datt_ref, grads_ref, vec_ref,
+    nf_ref, act_ref, dpre_ref, dbr_ref, dn_ref, acc_ref,
+):
+    vec_ref[...] = jnp.zeros_like(vec_ref)
+
+    @pl.loop(0, 4)
+    def _(t):
+        rows = pl.ds(pl.multiple_of(t * 256, 256), 256)
+        ctx = ctx_ref[rows, :]
+        res = tok_ref[rows, :].astype(F32) + dot_nn(ctx, wo_ref[...]) + ob_ref[...]
+        n, rstd = norm_parts(res)
+        normed = (n * g_ref[...] + s_ref[...]).astype(BF16)
+        nf_ref[rows, :] = normed
+        dy = cot_ref[rows, :]
+        acc_ref[...] = res + bb_ref[...]
+        dn_ref[...] = jnp.zeros_like(dn_ref)
+
+        @pl.loop(0, 4)
+        def _(c):
+            cut = pl.ds(pl.multiple_of(c * 768, 768), 768)
+            v = dot_nn(normed, wi_ref[:, cut]) + ib_ref[:, cut]
+            wb = wb_ref[cut, :]
+            d_act = dot_nt(dy, wb)
+            sq = v * v
+            th = jnp.tanh(v * (0.7978845608 + (0.7978845608 * 0.044715) * sq))
+            half = 0.5 + 0.5 * th
+            act = (v * half).astype(BF16)
+            slope = half + v * (half * (1.0 - th)) * (
+                0.7978845608 + (3 * 0.7978845608 * 0.044715) * sq
+            )
+            d_pre = (d_act * slope).astype(BF16)
+            act_ref[rows, cut] = act
+            dpre_ref[rows, cut] = d_pre
+            acc_ref[...] += dot_nn(act, wb)
+            dn_ref[...] += dot_nt(d_pre, wi_ref[:, cut])
+            vec_ref[pl.ds(4 + c, 1), :] += jnp.sum(d_pre.astype(F32), axis=0, keepdims=True)
+
+        out_ref[rows, :] = acc_ref[...].astype(BF16)
+        d_normed = dn_ref[...]
+        dyf = dy.astype(F32)
+        d_res = dyf + norm_back(d_normed, n, rstd, g_ref[...])
+        dres_ref[rows, :] = d_res
+        d_branch = d_res.astype(BF16)
+        dbr_ref[rows, :] = d_branch
+        datt_ref[rows, :] = dot_nt(d_branch, wo_ref[...]).astype(BF16)
+        vec_ref[0:1, :] += jnp.sum(dyf, axis=0, keepdims=True)
+        vec_ref[1:2, :] += jnp.sum(d_normed * n, axis=0, keepdims=True)
+        vec_ref[2:3, :] += jnp.sum(d_normed, axis=0, keepdims=True)
+        vec_ref[3:4, :] += jnp.sum(d_branch.astype(F32), axis=0, keepdims=True)
+
+    @pl.loop(0, 4)
+    def _(u):
+        cut = pl.ds(pl.multiple_of(u * 768, 768), 768)
+        g = dot_tn(nf_ref[...], dpre_ref[:, cut])
+        for r in range(32):
+            rows = slice(r * 24, (r + 1) * 24)
+            grads_ref[2 * u, place(r, 0)] = blocks_of(g[rows, :UW], g[rows, UW:])
+
+    g = dot_tn(ctx_ref[...], dbr_ref[...])
+    for r in range(32):
+        rows = slice(r * 24, (r + 1) * 24)
+        grads_ref[8, place(r, 0)] = blocks_of(g[rows, :UW], g[rows, UW:])
+
+    @pl.loop(0, 4)
+    def _(z):
+        g = dot_tn(act_ref[:, pl.ds(pl.multiple_of(z * 768, 768), 768)], cot_ref[...])
+        for r in range(8):
+            for i in range(2):
+                for j in range(2):
+                    block = g[r * 96 + i * 48 : r * 96 + i * 48 + 48, j * UW : (j + 1) * UW]
+                    grads_ref[4 * i + 2 * j + 1, place(r, 1) + z] = block.astype(BF16)
+
+
+def bwd_kernel(
+    len_ref, mask_ref, tok_ref, gain_ref, w_ref, nt_ref, q_ref, k_ref, v_ref, ctx_ref, lt_ref,
+    datt_ref, dres_ref,
+    dtok_ref, grads_ref, vec_ref,
+    dproj_ref, dq_ref, gq_ref, delta_ref,
+):
+    lane = lax.broadcasted_iota(jnp.int32, (1, 128), 1)
+    kpos = lax.broadcasted_iota(jnp.int32, (T, 1), 0)
+    valid = (kpos < len_ref[0]) & (mask_ref[...] == 1)
+    bias = jnp.where(valid, 0.0, NEG_FILL).astype(F32)
+    eye = lax.broadcasted_iota(jnp.int32, (256, 256), 0) == lax.broadcasted_iota(
+        jnp.int32, (256, 256), 1
+    )
+    head_of = lax.broadcasted_iota(jnp.int32, (8, 128), 1) // HD == lax.broadcasted_iota(
+        jnp.int32, (8, 128), 0
+    )
+    pick = jnp.where(head_of, 1.0, 0.0).astype(F32)
+    vec_ref[...] = jnp.zeros_like(vec_ref)
+
+    @pl.loop(0, 3)
+    def _(j):
+        for half in range(2):
+            p = 2 * j + half
+            cols = pl.ds(pl.multiple_of(p * 128, 128), 128)
+            qp, do = q_ref[:, cols], datt_ref[:, cols]
+            prod = do.astype(F32) * ctx_ref[:, cols].astype(F32)
+            delta = lax.dot_general(
+                pick, prod, (((1,), (1,)), ((), ())),
+                preferred_element_type=F32, precision=lax.Precision.HIGHEST,
+            )
+            delta_ref[...] = delta
+            dq_ref[...] = jnp.zeros_like(dq_ref)
+            for i in range(4):
+                cut = slice(i * 256, (i + 1) * 256)
+                kp, vp = k_ref[cut, cols], v_ref[cut, cols]
+                dks, dvs = [], []
+                for h in range(2):
+                    mine = (lane < HD) == (h == 0)
+                    kh = jnp.where(mine, kp, jnp.zeros_like(kp))
+                    vh = jnp.where(mine, vp, jnp.zeros_like(vp))
+                    raw = dot_nt(kh, qp)
+                    pieces = []
+                    for m in range(4):
+                        piece = raw[:, m * 256 : (m + 1) * 256] + bias[cut]
+                        if i == m:
+                            piece = jnp.where(eye, raw[:, m * 256 : (m + 1) * 256], piece)
+                        pieces.append(piece)
+                    s = jnp.concatenate(pieces, axis=1)
+                    e = jnp.exp(s - lt_ref[2 * p + h])
+                    dvs.append(dot_nn(e.astype(BF16), do))
+                    dp = dot_nt(vh, do)
+                    ds = (e * (dp - delta_ref[h : h + 1, :])).astype(BF16)
+                    dks.append(dot_nn(ds, qp))
+                    dq_ref[...] += dot_tn(ds, kh)
+                dproj_ref[3 * p + 1, cut] = jnp.where(lane < HD, dks[0], dks[1]).astype(BF16)
+                dproj_ref[3 * p + 2, cut] = jnp.where(lane < HD, dvs[0], dvs[1]).astype(BF16)
+            dproj_ref[3 * p] = dq_ref[...].astype(BF16) * jnp.asarray(0.125, BF16)
+            d3 = jnp.concatenate([dproj_ref[3 * p + n] for n in range(3)], axis=1)
+            vec_ref[0:1, cols] = jnp.sum(d3[:, :128].astype(F32), axis=0, keepdims=True)
+            vec_ref[1:2, cols] = jnp.sum(d3[:, 256:].astype(F32), axis=0, keepdims=True)
+            g = dot_nn(nt_ref[...], d3)
+            if half == 0:
+                gq_ref[...] = g
+            else:
+                for r in range(32):
+                    rows = slice(r * 24, (r + 1) * 24)
+                    grads_ref[j, place(r, (j + 1) % 2)] = blocks_of(gq_ref[rows, :], g[rows, :])
+
+    @pl.loop(0, 4)
+    def _(t):
+        rows = pl.ds(pl.multiple_of(t * 256, 256), 256)
+        dqs = jnp.concatenate([dproj_ref[3 * p, rows] for p in range(PAIRS)], axis=1)
+        dks = jnp.concatenate([dproj_ref[3 * p + 1, rows] for p in range(PAIRS)], axis=1)
+        dvs = jnp.concatenate([dproj_ref[3 * p + 2, rows] for p in range(PAIRS)], axis=1)
+        d_normed = (
+            dot_nt(dqs, w_ref[:, :D]) + dot_nt(dks, w_ref[:, D : 2 * D]) + dot_nt(dvs, w_ref[:, 2 * D :])
+        )
+        n, rstd = norm_parts(tok_ref[rows, :].astype(F32))
+        dtok_ref[rows, :] = dres_ref[rows, :] + norm_back(d_normed, n, rstd, gain_ref[...])
+        vec_ref[2:3, :] += jnp.sum(d_normed * n, axis=0, keepdims=True)
+        vec_ref[3:4, :] += jnp.sum(d_normed, axis=0, keepdims=True)
+
+
+def rs_kernel(
+    gf_ref, gq_ref, vf_ref, vb_ref,
+    gin_ref, gback_ref, gout_ref, gqkv_ref, vec_ref,
+    r0, r1, r2, r3, vs, vr,
+    s0, t0, s1, t1, s2, t2, s3, t3, sv, tv,
+):
+    dp, x = lax.axis_index("dp"), lax.axis_index("seq")
+    z, y, c = dp // 4, (dp // 2) % 2, dp % 2
+    over_c = (dp + 1 - 2 * c, x)
+    over_x = (dp, 1 - x)
+    over_y = (dp + 2 - 4 * y, x)
+    over_z = [(lax.rem(z + d, 4) * 4 + y * 2 + c, x) for d in (1, 2, 3)]
+    barrier = pltpu.get_barrier_semaphore()
+    for to in (over_c, over_x, over_y, *over_z):
+        pl.semaphore_signal(barrier, inc=1, device_id=to, device_id_type=MESH)
+    pl.semaphore_wait(barrier, 6)
+
+    def copy(src, dst, send, recv, to):
+        return pltpu.make_async_remote_copy(
+            src_ref=src, dst_ref=dst, send_sem=send, recv_sem=recv, device_id=to, device_id_type=MESH
+        )
+
+    def hop0(u, g, v):
+        return copy(g.at[v, pl.ds((1 - c) * 16, 16)], r0.at[u], s0.at[u], t0.at[u], over_c)
+
+    def axes(u):
+        fx = u % 2
+        first = (dp + (1 - fx) * (2 - 4 * y), x + fx * (1 - 2 * x))
+        second = (dp + fx * (2 - 4 * y), x + (1 - fx) * (1 - 2 * x))
+        return first, second, y + fx * (x - y), x + fx * (y - x)
+
+    def hop1(u):
+        first, _, a, _ = axes(u)
+        return copy(r0.at[u, pl.ds((1 - a) * 8, 8)], r1.at[u], s1.at[u], t1.at[u], first)
+
+    def hop2(u):
+        _, second, _, b = axes(u)
+        return copy(r1.at[u, pl.ds((1 - b) * 4, 4)], r2.at[u], s2.at[u], t2.at[u], second)
+
+    def hop3(u, d):
+        to = lax.rem(z + d + 1, 4)
+        return copy(r2.at[u, to], r3.at[u, d], s3.at[u, d], t3.at[u, d], over_z[d])
+
+    def vhop(n, to):
+        src = vs.at[min(n, 3)]
+        return copy(src, vr.at[n], sv.at[n], tv.at[n], to)
+
+    hops = [over_c, over_x, over_y, *over_z]
+    vs[0, :8] = vf_ref[...]
+    vs[0, 8:] = vb_ref[...]
+    vhop(0, hops[0]).start()
+
+    @pl.loop(0, 9)
+    def _(u):
+        hop0(u, gf_ref, u).start()
+
+    @pl.loop(0, 3)
+    def _(u):
+        hop0(u + 9, gq_ref, u).start()
+
+    def one(u, g, v):
+        hop0(u, g, v).wait_recv()
+
+        @pl.loop(0, 16)
+        def _(k):
+            r0[u, k] = (r0[u, k].astype(F32) + g[v, c * 16 + k].astype(F32)).astype(BF16)
+
+        hop1(u).start()
+
+    @pl.loop(0, 9)
+    def _(u):
+        one(u, gf_ref, u)
+
+    @pl.loop(0, 3)
+    def _(u):
+        one(u + 9, gq_ref, u)
+
+    for n in range(2):
+        vhop(n, hops[n]).wait_recv()
+        vs[n + 1] = vs[n] + vr[n]
+        vhop(n + 1, hops[n + 1]).start()
+
+    @pl.loop(0, UNITS)
+    def _(u):
+        hop1(u).wait_recv()
+        _, _, a, _ = axes(u)
+
+        @pl.loop(0, 8)
+        def _(k):
+            r1[u, k] = (r1[u, k].astype(F32) + r0[u, a * 8 + k].astype(F32)).astype(BF16)
+
+        hop2(u).start()
+
+    vhop(2, hops[2]).wait_recv()
+    vs[3] = vs[2] + vr[2]
+    for d in range(3):
+        vhop(3 + d, hops[3 + d]).start()
+
+    @pl.loop(0, UNITS)
+    def _(u):
+        hop2(u).wait_recv()
+        _, _, _, b = axes(u)
+
+        @pl.loop(0, 4)
+        def _(k):
+            r2[u, k] = (r2[u, k].astype(F32) + r1[u, b * 4 + k].astype(F32)).astype(BF16)
+
+        for d in range(3):
+            hop3(u, d).start()
+
+    for u in range(UNITS):
+        total = r2[u, z].astype(F32)
+        for d in range(3):
+            hop3(u, d).wait_recv()
+            total = total + r3[u, d].astype(F32)
+        if u == 8:
+            gout_ref[:, :UW] = total[:24]
+            gout_ref[:, UW:] = total[24:]
+        elif u > 8:
+            for half in range(2):
+                p = 2 * (u - 9) + half
+                for n in range(3):
+                    at = n * D + p * 128
+                    gqkv_ref[:, at : at + 128] = total[half * 24 : half * 24 + 24, n * 128 : n * 128 + 128]
+        elif u % 2 == 0:
+            at = (u // 2) * 768
+            gin_ref[:, at : at + UW] = total[:24]
+            gin_ref[:, at + UW : at + 2 * UW] = total[24:]
+        else:
+            i, j = u // 4, (u // 2) % 2
+            gback_ref[i * 48 : i * 48 + 48, j * UW : (j + 1) * UW] = total
+    total = vs[3]
+    for d in range(3):
+        vhop(3 + d, hops[3 + d]).wait_recv()
+        total = total + vr[3 + d]
+    vec_ref[...] = total
+
+    @pl.loop(0, 9)
+    def _(u):
+        hop0(u, gf_ref, u).wait_send()
+
+    @pl.loop(0, 3)
+    def _(u):
+        hop0(u + 9, gq_ref, u).wait_send()
+
+    @pl.loop(0, UNITS)
+    def _(u):
+        hop1(u).wait_send()
+        hop2(u).wait_send()
+        for d in range(3):
+            hop3(u, d).wait_send()
+
+    for n in range(6):
+        vhop(n, hops[n]).wait_send()
+
+
+VM = pl.BlockSpec(memory_space=pltpu.VMEM)
+SM = pl.BlockSpec(memory_space=pltpu.SMEM)
+
+
+def shape(dims, dtype):
+    return jax.ShapeDtypeStruct(dims, dtype)
+
+
+def call_fwd(length, mask, tok, gain, shift, w_qkv, qb, vb):
+    low = shape((T, D), BF16)
+    return pl.pallas_call(
+        fwd_kernel,
+        out_shape=(shape((D, T), BF16), low, low, low, low, shape((H, 1, T), F32)),
+        in_specs=[SM] + [VM] * 7,
+        out_specs=(VM,) * 6,
+        compiler_params=pltpu.CompilerParams(vmem_limit_bytes=VMEM_LIMIT),
+    )(length, mask, tok, gain, shift, w_qkv, qb, vb)
+
+
+def call_ffn(*args):
+    low = shape((T, D), BF16)
+    return pl.pallas_call(
+        ffn_kernel,
+        out_shape=(
+            low, shape((T, D), F32), low, shape((9, 32, 48, UW), BF16), shape((8, D), F32),
+        ),
+        in_specs=[VM] * 11,
+        out_specs=(VM,) * 5,
+        scratch_shapes=[
+            pltpu.VMEM((T, D), BF16),
+            pltpu.VMEM((T, FF), BF16),
+            pltpu.VMEM((T, FF), BF16),
+            pltpu.VMEM((T, D), BF16),
+            pltpu.VMEM((256, D), F32),
+            pltpu.VMEM((256, D), F32),
+        ],
+        compiler_params=pltpu.CompilerParams(vmem_limit_bytes=VMEM_LIMIT),
+    )(*args)
+
+
+def call_bwd(*args):
+    return pl.pallas_call(
+        bwd_kernel,
+        out_shape=(shape((T, D), F32), shape((3, 32, 48, UW), BF16), shape((8, D), F32)),
+        in_specs=[SM] + [VM] * 12,
+        out_specs=(VM,) * 3,
+        scratch_shapes=[
+            pltpu.VMEM((18, T, 128), BF16),
+            pltpu.VMEM((T, 128), F32),
+            pltpu.VMEM((D, UW), F32),
+            pltpu.VMEM((8, T), F32),
+        ],
+        compiler_params=pltpu.CompilerParams(vmem_limit_bytes=VMEM_LIMIT),
+    )(*args)
+
+
+def call_rs(gf, gq, vf, vb):
+    dma = pltpu.SemaphoreType.DMA
+    return pl.pallas_call(
+        rs_kernel,
+        out_shape=(
+            shape((24, FF), F32), shape((96, D), F32), shape((24, D), F32), shape((24, 3 * D), F32),
+            shape((16, D), F32),
+        ),
+        in_specs=[VM] * 4,
+        out_specs=(VM,) * 5,
+        scratch_shapes=[
+            pltpu.VMEM((UNITS, 16, 48, UW), BF16),
+            pltpu.VMEM((UNITS, 8, 48, UW), BF16),
+            pltpu.VMEM((UNITS, 4, 48, UW), BF16),
+            pltpu.VMEM((UNITS, 3, 48, UW), BF16),
+            pltpu.VMEM((4, 16, D), F32),
+            pltpu.VMEM((6, 16, D), F32),
+            dma((UNITS,)), dma((UNITS,)), dma((UNITS,)), dma((UNITS,)), dma((UNITS,)), dma((UNITS,)),
+            dma((UNITS, 3)), dma((UNITS, 3)), dma((6,)), dma((6,)),
+        ],
+        compiler_params=pltpu.CompilerParams(
+            vmem_limit_bytes=VMEM_LIMIT, collective_id=0, has_side_effects=True
+        ),
+    )(gf, gq, vf, vb)
+
+
+def whole_sequences(
+    tokens, lengths, key_mask, attn_gain, attn_shift, w_qkv, query_bias, value_bias, w_out,
+    out_bias, ffn_gain, ffn_shift, w_in, in_bias, w_back, back_bias, cotangent,
+):
+    x = lax.axis_index("seq")
+    swap = [(0, 1), (1, 0)]
+
+    def gather(rows):
+        own = lax.dynamic_index_in_dim(rows, x, 0, keepdims=False)
+        other = lax.dynamic_index_in_dim(rows, 1 - x, 0, keepdims=False)
+        got = lax.ppermute(other, "seq", swap)
+        return jnp.concatenate([jnp.where(x == 0, own, got), jnp.where(x == 0, got, own)], axis=0)
+
+    def spread(rows):
+        own = lax.dynamic_slice_in_dim(rows, x * HALF, HALF, 0)
+        other = lax.dynamic_slice_in_dim(rows, (1 - x) * HALF, HALF, 0).astype(BF16)
+        got = lax.ppermute(other, "seq", swap).astype(rows.dtype)
+        return jnp.stack([jnp.where(x == 0, own, got), jnp.where(x == 0, got, own)], axis=0)
+
+    def row(vector):
+        return vector.reshape(1, -1)
+
+    tok = gather(tokens)
+    mask = gather(key_mask)
+    length = lax.dynamic_slice_in_dim(lengths, x, 1)
+    normed_t, q, k, v, ctx, log_total = call_fwd(
+        length, row(mask), tok, row(attn_gain), row(attn_shift), w_qkv, row(query_bias), row(value_bias)
+    )
+    cotangent, _ = lax.optimization_barrier((cotangent, tok))
+    cot = gather(cotangent)
+    out, d_res, d_att, gf, vf = call_ffn(
+        tok, cot, ctx, w_out, row(out_bias), row(ffn_gain), row(ffn_shift), w_in, row(in_bias),
+        w_back, row(back_bias),
+    )
+    layer_out = spread(out)
+    d_tok, gq, vb = call_bwd(
+        length, mask.reshape(T, 1), tok, row(attn_gain), w_qkv, normed_t, q, k, v, ctx, log_total,
+        d_att, d_res,
+    )
+    grad_tokens = spread(d_tok)
+    g_in, g_back, g_out, g_qkv, vec = call_rs(gf, gq, vf, vb)
+    rank = lax.axis_index("dp") * 2 + x
+    mine = lax.dynamic_slice(vec, (0, rank * 24), (16, 24))
+    ib = lax.dynamic_slice(vec, (4 + rank // 8, (rank % 8) * 96), (1, 96)).reshape(96)
+    return (
+        layer_out, grad_tokens, mine[10], mine[11], g_qkv, mine[8], mine[9], g_out, mine[3],
+        mine[1], mine[2], g_in, ib, g_back, mine[0],
+    )
 
 
 def shifted(array, axis, by):
@@ -236,8 +784,10 @@
 
 
 def solution(mesh):
+    sizes = dict(mesh.shape)
+    whole = sizes == {"dp": 16, "seq": 2}
     return jax.shard_map(
-        shards,
+        whole_sequences if whole else shards,
         mesh=mesh,
         in_specs=(
             P("dp", "seq", None),

time: 778 us -> 323 us (0.42)
  waiting for transfers between devices: 295 us -> 28.7 us
  Pallas kernels: 0 us -> 260 us
  matrix products: 258 us -> 0 us
  local copies, waits for them, and re-layouts: 88.7 us -> 16.7 us
  other arithmetic: 67.9 us -> 8.71 us
  blocking collectives: 45.8 us -> 0 us
  between operations: 14.6 us -> 0.86 us
    pallas_call x0 -> x4, Pallas kernels: none -> 260 us  [the longest x1 119 us: call_rs(): pl.pallas_call(rs_kernel, out_shape=(shape((24, FF), F32), shape((96, D),...]
    dot_general x24 -> x0, matrix products: 258 us -> none  [the longest x4 37.5 us: outer_product(): lax.dot_general(left, right, (((0,), (0,)), ((), ())), preferred_element_...]
    ppermute x3 -> x5, waiting for transfers between devices: 151 us -> 28.7 us  [the longest x3 28.7 us: gather(): got = lax.ppermute(other, 'seq', swap)]
    reduce_scatter x4 -> x0, waiting for transfers between devices: 75 us -> none  [the longest x1 75 us: shards(): lax.psum_scatter(grad_w_qkv, ('dp', 'seq'), scatter_dimension=0, tiled=True)]
    all_gather x1 -> x0, waiting for transfers between devices: 68.8 us -> none  [shards(): lax.all_gather(keyval, 'seq', axis=1, tiled=True)]
    unnamed x1 -> x0, blocking collectives: 40.4 us -> none
    reduce_sum x10 -> x0, other arithmetic: 39.5 us -> none  [the longest x1 21.2 us: shards(): running_sum = jnp.sum(expo, axis=-1)]
    slice x8 -> x0, local copies, waits for them, and re-layouts: 27.1 us -> none  [the longest x3 13.2 us: split_block(): block_kv[:, :, :model_width].reshape(seq_count, key_count, H, HD)]
  transfers between devices with their start and end apart: 8 -> 5, of which waited for: 5 -> 2; matrix products, arithmetic and copies ran while one was open for 35% -> 4% of each run, Pallas kernels for 0% -> 46%
where the time goes in v1:
time: 323 us
  Pallas kernels  260 us (80%)
  waiting for transfers between devices  28.7 us (9%)
  local copies, waits for them, and re-layouts  16.7 us (5%)
  other arithmetic  8.71 us (3%)
  starting transfers between devices  7.43 us (2%)
    pallas_call x1, Pallas kernels, call_rs(): pl.pallas_call(rs_kernel, out_shape=(shape((24, FF), F32), shape((96, D),...  119 us
    pallas_call x1, Pallas kernels, call_bwd(): pl.pallas_call(bwd_kernel, out_shape=(shape((T, D), F32), shape((3, 32, 4...  57.3 us
    pallas_call x1, Pallas kernels, call_ffn(): pl.pallas_call(ffn_kernel, out_shape=(low, shape((T, D), F32), low, shape...  55.5 us
    ppermute x3, waiting for transfers between devices, gather(): got = lax.ppermute(other, 'seq', swap)  28.7 us
    pallas_call x1, Pallas kernels, call_fwd(): pl.pallas_call(fwd_kernel, out_shape=(shape((D, T), BF16), low, low, low,...  28.2 us
  transfers between devices with their start and end apart: 5, of which 2 were waited for; matrix products, arithmetic and copies ran while one was open for 4% of the time, Pallas kernels for 46%

profile of v1, /device:TPU:0, one launch (start us, length us, event | category | flops | bytes accessed | tf_op | source)
XLA Modules:
  0.0 322.7 jit_solution(11143247919246928513)
XLA Ops:
  0.7 1.3 dynamic-slice_bitcast_fusion.1
  2.0 3.0 collective-permute-start
  5.0 17.5 %collective-permute-done = bf16[512,768]{1,0:T(8,128)(2,1)S(1)} collective-permute-done((bf16[512,768]{1,0:T(8,128)(2,1)S(1)}, bf16[512,768]{1,0:T(8,128)(2,1)S(1)}, u32[]{:S(2)}, u32[]{:S(2)}) %collective-permute-start) | collective-permute-done | bytes 786464 | tf_op jit(solution)/shard_map/ppermute | solution.py:522
  22.5 0.1 bitcast_select_fusion.3
  22.6 0.0 copy-start.2
  22.6 1.2 pad_maximum_fusion.1.tok_ref
  23.9 0.7 copy-done.2
  24.6 0.0 copy-start.12
  24.6 0.0 copy-start.13
  24.6 0.0 copy-start.14
  24.7 0.0 copy-start.15
  24.7 0.0 copy-start.16
  24.7 0.0 copy-start.17
  24.7 0.1 dynamic-slice_bitcast_fusion
  24.8 1.8 collective-permute-start.1
  26.6 0.5 collective-permute-start.2
  27.1 0.6 dynamic_slice.45.len_ref
  27.7 0.6 reshape.68.gain_ref
  28.3 0.6 reshape.69.shift_ref
  28.9 0.6 reshape.70.qb_ref
  29.5 0.6 reshape.71.vb_ref
  30.1 0.6 reshape.72.ob_ref
  30.6 0.6 reshape.73.g_ref
  31.2 0.6 reshape.74.s_ref
  31.8 0.6 reshape.76.bb_ref
  32.4 11.2 %collective-permute-done.2 = s32[512]{0:T(512)S(1)} collective-permute-done((s32[512]{0:T(512)S(1)}, s32[512]{0:T(512)S(1)}, u32[]{:S(2)}, u32[]{:S(2)}) %collective-permute-start.2) | collective-permute-done | bytes 2080 | tf_op jit(solution)/shard_map/ppermute | solution.py:522
  43.6 1.0 copy.32.mask_ref
  44.6 28.2 %shard_map.280 = (bf16[768,1024]{1,0:T(8,128)(2,1)}, bf16[1024,768]{1,0:T(8,128)(2,1)}, bf16[1024,768]{1,0:T(8,128)(2,1)}, bf16[1024,768]{1,0:T(8,128)(2,1)}, bf...) custom-call(s32[1]{0:T(128)} %dynamic_slice.45.len_ref, s32[1,1024]{1,0:T(1,128)} %bitcast.42, ...), custom_call_target="tpu_custom_call" | custom-call | tf_op jit(solution)/shard_map/pallas_call | solution.py:440
  72.9 0.1 bitcast_select_fusion.1
  73.0 1.3 pad_maximum_fusion.2.cot_ref
  74.3 55.5 %shard_map.281 = (bf16[1024,768]{1,0:T(8,128)(2,1)}, f32[1024,768]{1,0:T(8,128)}, bf16[1024,768]{1,0:T(8,128)(2,1)}, bf16[9,32,48,384]{3,2,1,0:T(8,128)(2,1)}, f32[8,768]{1,0:T(8,128)}) custom-call(bf16[1024,768]{1,0:T(8,128)(2,1)} %pad_maximum_fusion.1.tok_ref, bf16[1024,768]{1,0:T(8,128)(2,1)} %pad_maximum_fusion.2.cot_ref, ...), custom_call_target="tpu_custom_call" | custom-call | tf_op jit(solution)/shard_map/pallas_call | solution.py:451
  129.8 57.3 %shard_map.282 = (f32[1024,768]{1,0:T(8,128)}, bf16[3,32,48,384]{3,2,1,0:T(8,128)(2,1)}, f32[8,768]{1,0:T(8,128)}) custom-call(s32[1]{0:T(128)} %dynamic_slice.45.len_ref, s32[1024,1]{1,0:T(8,128)} %copy.32.mask_ref, bf16[1024,768]{1,0:T(8,128)(2,1)} %pad_maximum_fusion.1.tok_ref, f32[1,768]{1,0:T(1,128)} %reshape.68.gain_ref, bf16[768,2304]{1,0:T(8,128)(2,1)} %w_ref.3, ...), custom_call_target="tpu_custom_call" | custom-call | tf_op jit(solution)/shard_map/pallas_call | solution.py:471
  187.1 2.5 dynamic-slice_convert_fusion
  189.5 1.4 collective-permute-start.4
  191.0 0.1 constant_dynamic-slice_fusion.1
  191.0 0.7 collective-permute-start.3
  191.7 119.2 %shard_map.283 = (f32[24,3072]{1,0:T(8,128)}, f32[96,768]{1,0:T(8,128)}, f32[24,768]{1,0:T(8,128)}, f32[24,2304]{1,0:T(8,128)}, f32[16,768]{1,0:T(8,128)}) custom-call(bf16[9,32,48,384]{3,2,1,0:T(8,128)(2,1)} %get-tuple-element.46.gf_ref, bf16[3,32,48,384]{3,2,1,0:T(8,128)(2,1)} %get-tuple-element.47.gq_ref, f32[8,768]{1,0:T(8,128)} %get-tuple-element.48.vf_ref, ...), custom_call_target="tpu_custom_call" | custom-call | tf_op jit(solution)/shard_map/pallas_call | solution.py:488
  310.9 1.3 dynamic-slice_bitcast_fusion.9
  312.2 1.6 fusion.2
  313.8 1.4 fusion
  315.2 1.9 pad_maximum_fusion
  317.0 0.1 copy-done.4
  317.2 1.4 select_bitcast_fusion.1
  318.7 1.3 pad_maximum_fusion.3
  320.0 0.7 copy.37
  320.6 0.6 copy.38
  321.3 0.7 copy.39
  322.0 0.7 copy.40
  (37 shorter events, 0.1 us)
Async XLA Ops:
  0.6 21.9 %copy-start.1 = (bf16[2,512,768]{2,1,0:T(8,128)(2,1)S(1)}, bf16[2,512,768]{2,1,0:T(8,128)(2,1)}, u32[]{:S(2)}) copy-start(bf16[2,512,768]{2,1,0:T(8,128)(2,1)} %param.17) | copy-start | bytes 4718596
  2.0 20.5 %collective-permute-start = (bf16[512,768]{1,0:T(8,128)(2,1)S(1)}, bf16[512,768]{1,0:T(8,128)(2,1)S(1)}, u32[]{:S(2)}, u32[]{:S(2)}) collective-permute-start(bf16[512,768]{1,0:T(8,128)(2,1)S(1)} %dynamic-slice_bitcast_fusion.1), channel_id=1, source_target_pairs={{0,1},{1,0},{2,3},{3,2},{4,5},{5,4},{6,7},{7,6},{8,9},{9,8},{10,11... | collective-permute-start | bytes 2359304 | tf_op jit(solution)/shard_map/ppermute | solution.py:522
  22.6 2.0 copy-start.2
  24.6 2.0 copy-start.18
  24.6 2.5 copy-start.19
  24.6 3.1 copy-start.10
  24.6 3.7 %copy-start.11 = (f32[768]{0:T(1024)S(1)}, f32[768]{0:T(1024)}, u32[]{:S(2)}) copy-start(f32[768]{0:T(1024)} %param.21) | copy-start | bytes 9220
  24.6 4.2 %copy-start.12 = (f32[768]{0:T(1024)S(1)}, f32[768]{0:T(1024)}, u32[]{:S(2)}) copy-start(f32[768]{0:T(1024)} %param.23) | copy-start | bytes 9220
  24.6 4.8 %copy-start.13 = (f32[768]{0:T(1024)S(1)}, f32[768]{0:T(1024)}, u32[]{:S(2)}) copy-start(f32[768]{0:T(1024)} %param.24) | copy-start | bytes 9220
  24.6 5.4 %copy-start.14 = (f32[768]{0:T(1024)S(1)}, f32[768]{0:T(1024)}, u32[]{:S(2)}) copy-start(f32[768]{0:T(1024)} %param.26) | copy-start | bytes 9220
  24.7 6.0 %copy-start.15 = (f32[768]{0:T(1024)S(1)}, f32[768]{0:T(1024)}, u32[]{:S(2)}) copy-start(f32[768]{0:T(1024)} %param.27) | copy-start | bytes 9220
  24.7 6.6 %copy-start.16 = (f32[768]{0:T(1024)S(1)}, f32[768]{0:T(1024)}, u32[]{:S(2)}) copy-start(f32[768]{0:T(1024)} %param.28) | copy-start | bytes 9220
  24.7 7.1 %copy-start.17 = (f32[768]{0:T(1024)S(1)}, f32[768]{0:T(1024)}, u32[]{:S(2)}) copy-start(f32[768]{0:T(1024)} %param.32) | copy-start | bytes 9220
  24.8 48.1 %collective-permute-start.1 = (bf16[512,768]{1,0:T(8,128)(2,1)S(1)}, bf16[512,768]{1,0:T(8,128)(2,1)S(1)}, u32[]{:S(2)}, u32[]{:S(2)}) collective-permute-start(bf16[512,768]{1,0:T(8,128)(2,1)S(1)} %dynamic-slice_bitcast_fusion), channel_id=1, source_target_pairs={{0,1},{1,0},{2,3},{3,2},{4,5},{5,4},{6,7},{7,6},{8,9},{9,8},{10,11... | collective-permute-start | bytes 2359304 | tf_op jit(solution)/shard_map/ppermute | solution.py:522
  26.6 17.0 %collective-permute-start.2 = (s32[512]{0:T(512)S(1)}, s32[512]{0:T(512)S(1)}, u32[]{:S(2)}, u32[]{:S(2)}) collective-permute-start(s32[512]{0:T(512)S(1)} %bitcast.45), channel_id=1, source_target_pairs={{0,1},{1,0},{2,3},{3,2},{4,5},{5,4},{6,7},{7,6},{8,9},{9,8},{10,11... | collective-permute-start | bytes 6152 | tf_op jit(solution)/shard_map/ppermute | solution.py:522
  43.6 1.0 copy-start.9
  187.1 3.9 %copy-start.3 = (bf16[1024,768]{1,0:T(8,128)(2,1)S(1)}, bf16[1024,768]{1,0:T(8,128)(2,1)}, u32[]{:S(2)}) copy-start(bf16[1024,768]{1,0:T(8,128)(2,1)} %get-tuple-element.37) | copy-start | bytes 4718596
  189.5 124.2 %collective-permute-start.4 = (bf16[512,768]{1,0:T(8,128)(2,1)}, bf16[512,768]{1,0:T(8,128)(2,1)}, u32[]{:S(2)}, u32[]{:S(2)}) collective-permute-start(bf16[512,768]{1,0:T(8,128)(2,1)} %dynamic-slice_convert_fusion), channel_id=1, source_target_pairs={{0,1},{1,0},{2,3},{3,2},{4,5},{5,4},{6,7},{7,6},{8,9},{9,8},{10,11... | collective-permute-start | bytes 2359304 | tf_op jit(solution)/shard_map/ppermute | solution.py:528
  191.0 126.0 %collective-permute-start.3 = (bf16[512,768]{1,0:T(8,128)(2,1)S(1)}, bf16[512,768]{1,0:T(8,128)(2,1)}, u32[]{:S(2)}, u32[]{:S(2)}) collective-permute-start(bf16[512,768]{1,0:T(8,128)(2,1)S(1)} %constant_dynamic-slice_fusion.1), channel_id=1, source_target_pairs={{0,1},{1,0},{2,3},{3,2},{4,5},{5,4},{6,7},{7,6},{8,9},{9,8},{10,11... | collective-permute-start | bytes 2359304 | tf_op jit(solution)/shard_map/ppermute | solution.py:528
  191.7 122.1 %copy-start = (f32[1024,768]{1,0:T(8,128)S(1)}, f32[1024,768]{1,0:T(8,128)}, u32[]{:S(2)}) copy-start(f32[1024,768]{1,0:T(8,128)} %get-tuple-element.45) | copy-start | bytes 9437188
  315.2 2.0 copy-start.4
  318.6 1.3 copy-start.7
  318.6 2.0 copy-start.8
  318.7 2.6 copy-start.6
  318.7 3.3 %copy-start.5 = (f32[96,768]{1,0:T(8,128)S(1)}, f32[96,768]{1,0:T(8,128)}, u32[]{:S(2)}) copy-start(f32[96,768]{1,0:T(8,128)} %get-tuple-element.103) | copy-start | bytes 884740
